TPU v7x, 32 devices: a whole 2x2x4 slice. The times are simulated.
32 devices in a mesh: groups: 2 (over x), ex: 16 (over z, y, core).
Axes of the slice: x: 2, y: 2, z: 4, core: 2. Of those that a mesh axis runs over, the one named last changes fastest.
Arguments:
- tiles: bfloat16 [128, 32, 128, 128], P(('groups', 'ex')), parts along dimension 0, may hold values from -1.5 to 1.5
- column_blocks: int32 [128, 32], P(('groups', 'ex')), parts along dimension 0, may hold values from 0 to 8191
- occupied: int32 [128, 32], P(('groups', 'ex')), parts along dimension 0, may hold values 0 or 1
- labels: int32 [128, 128], P(('groups', 'ex')), parts along dimension 0, may hold values from -1 to 1, as said below
- weights: float32 [16384, 128], P(('groups', 'ex')), parts along dimension 0, may hold values from -0.6 to 0.6
Outputs:
- newton_step: float32 [16384, 128], P(('groups', 'ex')), parts along dimension 0
- residual: float32 [16384, 128], P(('groups', 'ex')), parts along dimension 0
There are 2 independent parts, one for each index of `groups`. A program takes and returns all parts, laid end to end along the dimension named above; each array names one. Nothing has to cross between parts.
Inputs may be any that keep to these rules, and one draw needn't show every extreme that they name: `labels`: each label is -1 or +1, never 0.
All inputs are finite; a program needn't handle non-finite values. No bound on the sum of `occupied` on one device may be relied on, other than what follows from the above.
Results may differ from a plain program's by a relative error of at most 0.012.
The roundings to bfloat16 on the way count: a program that leaves them out, or rounds other values in their place, can miss the bound.
Values may be sent and summed in bfloat16 or wider, within the bound.
No kernel may reach another device: no remote copies, remote signals or barrier semaphores. Data moves between devices by JAX's collectives and lax.ppermute only.
A program may use at most 64 MiB of HBM per device.

v0:
```python
import jax
import jax.numpy as jnp
from jax import lax
from jax.sharding import PartitionSpec as P

ITERS = 3


ridge = 1.0


def apply_picked(tiles, occupancy, picked):
    picked = picked * occupancy[:, :, None]
    return jnp.einsum("bkij,bkj->bi", tiles, picked, preferred_element_type=jnp.float32)


def tile_terms(tiles, occupancy, values):
    contrib = jnp.einsum("bkij,bi->bkj", tiles, values, preferred_element_type=jnp.float32)
    contrib = contrib * occupancy[:, :, None].astype(jnp.float32)
    return contrib.reshape(-1, tiles.shape[3])


def local(tiles, column_blocks, occupied, labels, weights):
    per_dev = weights.shape[0]
    all_blocks = per_dev * lax.axis_size("ex")
    flat_blocks = column_blocks.reshape(-1)
    occupancy = occupied.astype(jnp.bfloat16)
    signs = labels.astype(jnp.float32)
    full_weights = lax.all_gather(weights.astype(jnp.bfloat16), "ex", axis=0, tiled=True)
    picked_weights = full_weights[column_blocks]
    margins = apply_picked(tiles, occupancy, picked_weights)
    prob = jax.nn.sigmoid(-signs * margins)
    curv = prob * (1.0 - prob)
    slopes = (-signs * prob).astype(jnp.bfloat16)
    squares = tiles * tiles
    grad_terms = tile_terms(tiles, occupancy, slopes)
    diag_terms = tile_terms(squares, occupancy, curv.astype(jnp.bfloat16))
    grad_part = jax.ops.segment_sum(grad_terms, flat_blocks, num_segments=all_blocks)
    diag_part = jax.ops.segment_sum(diag_terms, flat_blocks, num_segments=all_blocks)
    grad_sum, diag_sum = (
        lax.psum_scatter(grad_part, "ex", scatter_dimension=0, tiled=True),
        lax.psum_scatter(diag_part, "ex", scatter_dimension=0, tiled=True),
    )
    gradient = grad_sum + ridge * weights
    precond = diag_sum + ridge
    newton_step = jnp.zeros_like(weights)
    residual = -gradient
    scaled = residual / precond
    direction = scaled
    res_dot = lax.psum(jnp.sum(residual * scaled), "ex")
    for step in range(ITERS):
        full_direction = lax.all_gather(direction.astype(jnp.bfloat16), "ex", axis=0, tiled=True)
        picked_direction = full_direction[column_blocks]
        moved = apply_picked(tiles, occupancy, picked_direction)
        terms = tile_terms(tiles, occupancy, (curv * moved).astype(jnp.bfloat16))
        dense_part = jax.ops.segment_sum(terms, flat_blocks, num_segments=all_blocks)
        image = lax.psum_scatter(dense_part, "ex", scatter_dimension=0, tiled=True)
        image = image + ridge * direction
        curvature = lax.psum(jnp.sum(direction * image), "ex")
        alpha = res_dot / curvature
        newton_step = newton_step + alpha * direction
        residual = residual - alpha * image
        scaled = residual / precond
        if step + 1 < ITERS:
            next_dot = lax.psum(jnp.sum(residual * scaled), "ex")
            direction = scaled + next_dot / res_dot * direction
            res_dot = next_dot
    return (newton_step, residual)


def solution(mesh):
    placed = (
        P(("groups", "ex"), None, None, None),
        P(("groups", "ex"), None),
        P(("groups", "ex"), None),
        P(("groups", "ex"), None),
        P(("groups", "ex"), None),
    )
    return jax.shard_map(
        local,
        mesh=mesh,
        in_specs=placed,
        out_specs=(P(("groups", "ex"), None), P(("groups", "ex"), None)),
        check_vma=False,
    )
```

profile of v0, /device:TPU:0, one launch (start us, length us, event | category | flops | bytes accessed | tf_op | source)
XLA Modules:
  0.0 753.6 jit_solution(286153695360985735)
XLA Ops:
  7.2 0.0 all-gather.5.cloned.1.call-start
  7.2 1.6 convert_element_type.42
  8.9 0.0 reduce-scatter.8.cloned.1.call-start
  8.9 0.8 reshape.61
  9.7 0.7 compare_select_fusion
  10.4 0.1 reshape.29
  10.5 0.7 fusion.37
  11.1 43.7 %all-gather.5.cloned.1.call-done = bf16[8192,128]{1,0:T(8,128)(2,1)} async-done(((bf16[512,128]{1,0:T(8,128)(2,1)}), bf16[8192,128]{1,0:T(8,128)(2,1)}) %all-gather.5.cloned.1.call-update) | async-done | bytes 2097168 | tf_op jit(solution)/shard_map/all_gather | solution.py:29
  54.9 2.5 gather_fusion
  57.4 0.1 multiply_bitcast_fusion.3
  57.5 3.5 fusion.18
  61.1 0.7 fusion
  61.7 0.7 fusion.27
  62.4 0.1 broadcast_multiply_fusion.4
  62.5 3.2 scatter_custom_fusion.1
  65.6 0.0 reduce-scatter.6.cloned.1.call-start
  65.7 3.2 scatter_custom_fusion
  68.9 0.0 reduce-scatter.6.cloned.1.call-update
  68.9 0.0 all-gather.7.cloned.1.call-start
  69.0 68.0 %reduce-scatter.8.cloned.1.call-done = f32[512,128]{1,0:T(8,128)} async-done(((f32[8192,128]{1,0:T(8,128)}), f32[512,128]{1,0:T(8,128)}) %reduce-scatter.8.cloned.1.call-update) | async-done | bytes 262160 | tf_op jit(solution)/shard_map/reduce_scatter | solution.py:42
  136.9 75.8 %reduce-scatter.6.cloned.1.call-done = f32[512,128]{1,0:T(8,128)} async-done(((f32[8192,128]{1,0:T(8,128)}), f32[512,128]{1,0:T(8,128)}) %reduce-scatter.6.cloned.1.call-update) | async-done | bytes 262160 | tf_op jit(solution)/shard_map/reduce_scatter | solution.py:41
  212.7 1.8 fusion.34
  214.5 0.0 reduce-scatter.10.cloned.1.call-start
  214.6 41.3 %all-gather.7.cloned.1.call-done = bf16[8192,128]{1,0:T(8,128)(2,1)} async-done(((bf16[512,128]{1,0:T(8,128)(2,1)}), bf16[8192,128]{1,0:T(8,128)(2,1)}) %all-gather.7.cloned.1.call-update) | async-done | bytes 2097168 | tf_op jit(solution)/shard_map/all_gather | solution.py:52
  255.9 2.5 gather_fusion.1
  258.4 0.1 multiply_bitcast_fusion.2
  258.5 3.5 fusion.16
  262.0 0.7 fusion.24
  262.7 0.1 broadcast_multiply_fusion.2
  262.8 3.2 scatter_custom_fusion.2
  265.9 0.0 all-gather.9.cloned.1.call-start
  266.0 71.3 %reduce-scatter.10.cloned.1.call-done = f32[512,128]{1,0:T(8,128)} async-done(((f32[8192,128]{1,0:T(8,128)}), f32[512,128]{1,0:T(8,128)}) %reduce-scatter.10.cloned.1.call-update) | async-done | bytes 262160 | tf_op jit(solution)/shard_map/reduce_scatter | solution.py:57
  337.3 1.6 multiply_reduce_fusion.4
  339.0 30.6 %all-reduce = (f32[]{:T(128)}, f32[]{:T(128)}) all-reduce(f32[]{:T(128)} %get-tuple-element.3, f32[]{:T(128)} %get-tuple-element.2), channel_id=1, replica_groups=mesh['groups'=2,'ex'=16] {'ex'}, use_global_device_ids=true, to_apply=%region_5.0 | all-reduce | flops 2 | bytes 16 | tf_op jit(solution)/shard_map/psum | solution.py:50
  371.0 1.7 multiply_reduce_fusion.3
  372.6 30.1 %psum.44 = f32[]{:T(128)} all-reduce(f32[]{:T(128)} %multiply_reduce_fusion.3), channel_id=1, replica_groups=mesh['groups'=2,'ex'=16] {'ex'}, use_global_device_ids=true, to_apply=%region_11.0 | all-reduce | flops 1 | bytes 8 | tf_op jit(solution)/shard_map/psum | solution.py:65
  403.9 1.7 fusion.36
  405.7 0.0 reduce-scatter.12.cloned.1.call-start
  405.7 38.8 %all-gather.9.cloned.1.call-done = bf16[8192,128]{1,0:T(8,128)(2,1)} async-done(((bf16[512,128]{1,0:T(8,128)(2,1)}), bf16[8192,128]{1,0:T(8,128)(2,1)}) %all-gather.9.cloned.1.call-update) | async-done | bytes 2097168 | tf_op jit(solution)/shard_map/all_gather | solution.py:52
  444.5 2.5 gather_fusion.2
  447.0 0.1 multiply_bitcast_fusion.1
  447.1 3.5 fusion.14
  450.6 0.7 fusion.22
  451.3 0.1 broadcast_multiply_fusion.1
  451.4 3.2 scatter_custom_fusion.3
  454.6 0.0 all-gather.11.cloned.1.call-start
  454.6 71.2 %reduce-scatter.12.cloned.1.call-done = f32[512,128]{1,0:T(8,128)} async-done(((f32[8192,128]{1,0:T(8,128)}), f32[512,128]{1,0:T(8,128)}) %reduce-scatter.12.cloned.1.call-update) | async-done | bytes 262160 | tf_op jit(solution)/shard_map/reduce_scatter | solution.py:57
  525.9 1.6 multiply_reduce_fusion.2
  527.5 30.8 %psum.45 = f32[]{:T(128)} all-reduce(f32[]{:T(128)} %get-tuple-element.12), channel_id=1, replica_groups=mesh['groups'=2,'ex'=16] {'ex'}, use_global_device_ids=true, to_apply=%region_15.0 | all-reduce | flops 1 | bytes 8 | tf_op jit(solution)/shard_map/psum | solution.py:59
  559.5 0.7 multiply_reduce_fusion.1
  560.2 30.1 %psum.46 = f32[]{:T(128)} all-reduce(f32[]{:T(128)} %get-tuple-element.10), channel_id=1, replica_groups=mesh['groups'=2,'ex'=16] {'ex'}, use_global_device_ids=true, to_apply=%region_17.0 | all-reduce | flops 1 | bytes 8 | tf_op jit(solution)/shard_map/psum | solution.py:65
  591.5 0.7 fusion.35
  592.3 0.2 reduce-scatter.14.cloned.1.call-start
  592.5 38.6 %all-gather.11.cloned.1.call-done = bf16[8192,128]{1,0:T(8,128)(2,1)} async-done(((bf16[512,128]{1,0:T(8,128)(2,1)}), bf16[8192,128]{1,0:T(8,128)(2,1)}) %all-gather.11.cloned.1.call-update) | async-done | bytes 2097168 | tf_op jit(solution)/shard_map/all_gather | solution.py:52
  631.1 2.5 gather_fusion.3
  633.6 0.1 multiply_bitcast_fusion
  633.7 3.5 fusion.12
  637.3 0.7 fusion.20
  637.9 0.1 broadcast_multiply_fusion
  638.0 3.2 scatter_custom_fusion.4
  641.2 71.4 %reduce-scatter.14.cloned.1.call-done = f32[512,128]{1,0:T(8,128)} async-done(((f32[8192,128]{1,0:T(8,128)}), f32[512,128]{1,0:T(8,128)}) %reduce-scatter.14.cloned.1.call-update) | async-done | bytes 262160 | tf_op jit(solution)/shard_map/reduce_scatter | solution.py:57
  712.6 1.6 multiply_reduce_fusion
  714.2 30.6 %psum.47 = f32[]{:T(128)} all-reduce(f32[]{:T(128)} %get-tuple-element.6), channel_id=1, replica_groups=mesh['groups'=2,'ex'=16] {'ex'}, use_global_device_ids=true, to_apply=%region_21.0 | all-reduce | flops 1 | bytes 8 | tf_op jit(solution)/shard_map/psum | solution.py:59
  746.2 0.9 multiply_subtract_fusion
  (30 shorter events, 0.2 us)
Async XLA Ops:
  7.2 53.8 %copy-start.7 = (s32[4,128]{1,0:T(4,128)S(1)}, s32[4,128]{1,0:T(4,128)}, u32[]{:S(2)}) copy-start(s32[4,128]{1,0:T(4,128)} %param.8) | copy-start | bytes 6148
  7.2 47.7 %all-gather.5.cloned.1.call-start = ((), (), s32[]{:S(2)}) async-start(), calls=%async_computation.5 | async-start | bytes 2228224 | tf_op jit(solution)/shard_map/all_gather | solution.py:29
  8.9 128.1 %reduce-scatter.8.cloned.1.call-start = ((), (), s32[]{:S(2)}) async-start(), calls=%async_computation.7 | async-start | bytes 4456448 | tf_op jit(solution)/shard_map/reduce_scatter | solution.py:42
  57.4 3.7 copy-start
  65.6 147.1 %reduce-scatter.6.cloned.1.call-start = ((), (), s32[]{:S(2)}) async-start(), calls=%async_computation.6 | async-start | bytes 4456448 | tf_op jit(solution)/shard_map/reduce_scatter | solution.py:41
  65.7 147.0 %copy-start.6 = (f32[512,128]{1,0:T(8,128)S(1)}, f32[512,128]{1,0:T(8,128)}, u32[]{:S(2)}) copy-start(f32[512,128]{1,0:T(8,128)} %param.9) | copy-start | bytes 786436
  68.9 186.9 %all-gather.7.cloned.1.call-start = ((), (), s32[]{:S(2)}) async-start(), calls=%async_computation.8 | async-start | bytes 2228224 | tf_op jit(solution)/shard_map/all_gather | solution.py:52
  214.5 122.8 %reduce-scatter.10.cloned.1.call-start = ((), (), s32[]{:S(2)}) async-start(), calls=%async_computation.9 | async-start | bytes 4456448 | tf_op jit(solution)/shard_map/reduce_scatter | solution.py:57
  258.4 3.6 copy-start.1
  262.8 74.6 %copy-start.4 = (f32[512,128]{1,0:T(8,128)S(1)}, f32[512,128]{1,0:T(8,128)}, u32[]{:S(2)}) copy-start(f32[512,128]{1,0:T(8,128)} %reduce-scatter.8.cloned.1.call-done) | copy-start | bytes 786436
  265.9 178.6 %all-gather.9.cloned.1.call-start = ((), (), s32[]{:S(2)}) async-start(), calls=%async_computation.10 | async-start | bytes 2228224 | tf_op jit(solution)/shard_map/all_gather | solution.py:52
  405.7 120.2 %reduce-scatter.12.cloned.1.call-start = ((), (), s32[]{:S(2)}) async-start(), calls=%async_computation.11 | async-start | bytes 4456448 | tf_op jit(solution)/shard_map/reduce_scatter | solution.py:57
  447.0 3.6 copy-start.2
  451.4 108.1 %copy-start.5 = (f32[512,128]{1,0:T(8,128)S(1)}, f32[512,128]{1,0:T(8,128)}, u32[]{:S(2)}) copy-start(f32[512,128]{1,0:T(8,128)} %reduce-scatter.10.cloned.1.call-done) | copy-start | bytes 786436
  454.6 176.5 %all-gather.11.cloned.1.call-start = ((), (), s32[]{:S(2)}) async-start(), calls=%async_computation.12 | async-start | bytes 2228224 | tf_op jit(solution)/shard_map/all_gather | solution.py:52
  592.3 120.3 %reduce-scatter.14.cloned.1.call-start = ((), (), s32[]{:S(2)}) async-start(), calls=%async_computation.13 | async-start | bytes 4456448 | tf_op jit(solution)/shard_map/reduce_scatter | solution.py:57
  633.6 3.6 copy-start.3
Sparse Core Ops, SparseCore 0:
  10.7 44.0 all-gather.4
  65.8 71.1 reduce-scatter.7
  141.3 71.3 reduce-scatter.5
  215.3 40.4 all-gather.6
  266.1 71.2 reduce-scatter.9
  405.8 38.6 all-gather.8
  454.7 71.1 reduce-scatter.11
  592.4 38.6 all-gather.10
  641.3 71.2 reduce-scatter.13
where the time goes:
time: 754 us
  waiting for transfers between devices  520 us (69%)
  blocking collectives  152 us (20%)
  other arithmetic  31.9 us (4%)
  between operations  20.4 us (3%)
  matrix products  17.4 us (2%)
  local copies, waits for them, and re-layouts  10.9 us (1%)
    reduce_scatter x3, waiting for transfers between devices, local(): image = lax.psum_scatter(dense_part, 'ex', scatter_dimension=0, tiled=True)  214 us
    all_gather x3, waiting for transfers between devices, local(): lax.all_gather(direction.astype(jnp.bfloat16), 'ex', axis=0, tiled=True)  119 us
    reduce_scatter x1, waiting for transfers between devices, local(): lax.psum_scatter(grad_part, 'ex', scatter_dimension=0, tiled=True)  75.8 us
    reduce_scatter x1, waiting for transfers between devices, local(): lax.psum_scatter(diag_part, 'ex', scatter_dimension=0, tiled=True)  68 us
    psum x2, blocking collectives, local(): curvature = lax.psum(jnp.sum(direction * image), 'ex')  61.4 us
    psum x2, blocking collectives, local(): next_dot = lax.psum(jnp.sum(residual * scaled), 'ex')  60.2 us
    all_gather x1, waiting for transfers between devices, local(): lax.all_gather(weights.astype(jnp.bfloat16), 'ex', axis=0, tiled=True)  43.7 us
    psum x1, blocking collectives, local(): res_dot = lax.psum(jnp.sum(residual * scaled), 'ex')  30.6 us
  transfers between devices with their start and end apart: 9, of which 9 were waited for; matrix products, arithmetic and copies ran while one was open for 1% of the time, Pallas kernels for 0%

commit v1 on v0

v1 whole, which is shorter than its diff:
```python
import functools

import jax
import jax.numpy as jnp
from jax import lax
from jax.experimental import pallas as pl
from jax.experimental.pallas import tpu as pltpu
from jax.sharding import PartitionSpec as P

RIDGE = 1.0
TAIL = 16
DIGIT = 128.0
F32 = jnp.float32
BF16 = jnp.bfloat16
VMEM = pl.BlockSpec(memory_space=pltpu.VMEM)
ANY = pl.BlockSpec(memory_space=pl.ANY)


def iota(shape, axis):
    return lax.broadcasted_iota(jnp.int32, shape, axis)


def params():
    return pltpu.CompilerParams(vmem_limit_bytes=40 * 1024 * 1024)


def swap(x, first, second=None):
    n = lax.axis_size("ex")
    second = first if second is None else second
    return lax.ppermute(x, "ex", [(i, i ^ (second if i % 2 else first)) for i in range(n)])


def gather_blocks(x):
    n = lax.axis_size("ex")
    pair = jnp.concatenate([x, swap(x, 1)], axis=0)
    chips = list(range(2, n, 2))
    blocks = [pair]
    split = [swap(pair, a, b) for a, b in zip(chips[0:-1:2], chips[1::2])]
    if len(chips) % 2:
        blocks.append(swap(pair, chips[-1]))
    for got in split:
        blocks += [got, swap(got, 1)]
    return blocks


def gather_wide(x):
    n = lax.axis_size("ex")
    across = [(s, swap(x, s)) for s in range(4, n, 4)]
    blocks = [(0, x), (2, swap(x, 2))] + across + [(s ^ 2, swap(got, 2)) for s, got in across]
    return blocks + [(s ^ 1, swap(got, 1)) for s, got in blocks]


def rounded(x):
    return x.astype(BF16).astype(F32)


def ids_of(tail):
    tail = tail.astype(F32)
    return tail[0:1] * DIGIT + tail[1:2]


def pieces(x):
    high = rounded(x)
    mid = rounded(x - high)
    return high, mid, x - high - mid


def tail_with(idtail, scalars):
    lanes = iota((1, idtail.shape[1]), 1)
    row = jnp.zeros((1, idtail.shape[1]), F32)
    for at, value in enumerate(scalars):
        row = jnp.where(lanes == at, value, row)
    out, rows = idtail, iota(idtail.shape, 0)
    for at, piece in enumerate(pieces(row)):
        out = jnp.where(rows == 2 + at, piece, out)
    return out.astype(BF16)


def total(x):
    return jnp.sum(jnp.sum(x, axis=0, keepdims=True), axis=1, keepdims=True)


def lane(row, at):
    return jnp.sum(jnp.where(iota(row.shape, 1) == at, row, 0.0), axis=1, keepdims=True)


def start_tiles(tiles_hbm, tiles, sems):
    copies = [pltpu.make_async_copy(tiles_hbm.at[b], tiles.at[b], sems.at[b]) for b in range(tiles.shape[0])]
    for copy in copies:
        copy.start()
    return copies


def rows_times(tiles, b, vec):
    k_all = tiles.shape[1]

    def body(k, acc):
        return acc + tiles[b, k].astype(F32) * vec[pl.ds(b * k_all + k, 1), :]

    acc = lax.fori_loop(0, k_all, body, jnp.zeros(tiles.shape[2:], F32), unroll=8)
    return jnp.sum(acc, axis=1, keepdims=True)


def columns_times(tiles, b, u, out):
    k_all = tiles.shape[1]

    def body(k, carry):
        out[pl.ds(b * k_all + k, 1), :] = jnp.sum(tiles[b, k].astype(F32) * u, axis=0, keepdims=True)
        return carry

    lax.fori_loop(0, k_all, body, 0, unroll=8)


def prep_kernel(cols_ref, occ_ref, w_ref, payload_ref, ccol_ref, idtail_ref):
    per, width = w_ref.shape
    payload_ref[0:per, :] = w_ref[...].astype(BF16)
    ids = jnp.where(occ_ref[...] > 0, cols_ref[...], -1).astype(F32)
    rows, k_all = ids.shape
    row = jnp.concatenate([ids[r : r + 1] for r in range(rows)], axis=1)
    high = jnp.floor(row * (1.0 / DIGIT))
    low = row - high * DIGIT
    at = iota((TAIL, width), 0)
    tail = jnp.where(at == 0, high, jnp.where(at == 1, low, 0.0))
    idtail_ref[...] = tail
    payload_ref[per : per + TAIL, :] = tail.astype(BF16)
    ccol_ref[...] = jnp.transpose(jnp.broadcast_to(row, (width, width)))


def first_kernel(xors, me_ref, *refs):
    n = len(xors)
    blocks = refs[:n]
    ccol_ref, idtail_ref, labels_ref, tiles_hbm = refs[n : n + 4]
    payload_ref, wslot_ref, curv_ref, grad_ref = refs[n + 4 : n + 8]
    tiles, tg, td, sems = refs[n + 8 :]
    copies = start_tiles(tiles_hbm, tiles, sems)
    slots, width = ccol_ref.shape
    per = blocks[0].shape[0] - TAIL
    r_all, k_all = tiles.shape[:2]
    me = me_ref[0]
    ccol = ccol_ref[...]
    occupied = ccol >= 0.0
    acc = jnp.zeros((slots, width), F32)
    for xor, block in zip(xors, blocks):
        base = ((me ^ xor) * per).astype(F32)
        at = ccol - base
        hot = jnp.concatenate(
            [(at == (iota((slots, width), 1) + q * width).astype(F32)).astype(F32).astype(BF16) for q in range(per // width)],
            axis=1,
        )
        acc = acc + jnp.dot(hot, block[0:per, :], preferred_element_type=F32)
    wslot_ref[...] = acc
    for b in range(r_all):
        copies[b].wait()
        margin = rows_times(tiles, b, wslot_ref)
        sign = jnp.transpose(jnp.broadcast_to(labels_ref[b : b + 1, :].astype(F32), (width, width)))
        prob = jax.nn.sigmoid(-sign * margin)
        curv = prob * (1.0 - prob)
        curv_ref[b] = curv
        slope = rounded(-sign * prob)
        weight = rounded(curv)

        def body(k, carry):
            x = tiles[b, k]
            tg[pl.ds(b * k_all + k, 1), :] = jnp.sum(x.astype(F32) * slope, axis=0, keepdims=True)
            td[pl.ds(b * k_all + k, 1), :] = jnp.sum((x * x).astype(F32) * weight, axis=0, keepdims=True)
            return carry

        lax.fori_loop(0, k_all, body, 0, unroll=4)
    grad = jnp.where(occupied, tg[...], 0.0)
    grad_ref[...] = grad
    payload_ref[0:slots, :] = grad.astype(BF16)
    payload_ref[slots : 2 * slots, :] = jnp.where(occupied, td[...], 0.0).astype(BF16)
    payload_ref[2 * slots : 2 * slots + TAIL, :] = idtail_ref[...].astype(BF16)


def apply_and_pack(copies, tiles, ccol, z, zrows, terms, curv_ref, weight, more, payload_ref, terms_ref, idtail_ref, res):
    slots = ccol.shape[0]
    zrows[...] = z
    quad = jnp.zeros((1, 1), F32)
    for b in range(tiles.shape[0]):
        if copies is not None:
            copies[b].wait()
        moved = rows_times(tiles, b, zrows)
        u = curv_ref[b] * moved
        quad = quad + jnp.sum(u[:, 0:1] * moved, axis=0, keepdims=True)
        columns_times(tiles, b, u, terms)
    found = jnp.where(ccol >= 0.0, terms[...], 0.0)
    terms_ref[...] = found
    payload_ref[0:slots, :] = found.astype(BF16)
    at = payload_ref.shape[0] - TAIL
    scalars = [total(weight * res * z), total(weight * z * z) + quad] + more
    payload_ref[at : at + TAIL, :] = tail_with(idtail_ref[...], scalars)


def hot_of(ccol, block, at):
    return (ccol == ids_of(block[at : at + TAIL, :])).astype(F32)


def start_kernel(n, *refs):
    blocks = refs[:n]
    ccol_ref, idtail_ref, wslot_ref, curv_ref, part_ref, tiles_hbm = refs[n : n + 6]
    payload_ref, m_ref, r_ref, z_ref, weight_ref, terms_ref = refs[n + 6 : n + 12]
    tiles, zrows, terms, sems = refs[n + 12 :]
    copies = start_tiles(tiles_hbm, tiles, sems)
    ccol = ccol_ref[...]
    slots, width = ccol.shape
    each = 2 * slots + TAIL
    acc = jnp.zeros((slots, 2 * width), F32)
    count = jnp.zeros((slots, width), F32)
    for block in blocks:
        for at in range(0, block.shape[0], each):
            hot = hot_of(ccol, block, at + 2 * slots)
            count = count + hot
            both = jnp.concatenate([block[at : at + slots, :], block[at + slots : at + 2 * slots, :]], axis=1)
            acc = acc + jnp.dot(hot.astype(BF16), both, preferred_element_type=F32)
    weight = 1.0 / jnp.sum(count, axis=1, keepdims=True)
    weight_ref[...] = jnp.broadcast_to(weight, (slots, width))
    m = acc[:, width:] + RIDGE
    r = -(acc[:, :width] + RIDGE * wslot_ref[...])
    z = r / m
    m_ref[...] = m
    r_ref[...] = r
    z_ref[...] = z
    apply_and_pack(
        copies, tiles, ccol, z, zrows, terms, curv_ref, weight, [jnp.zeros((1, 1), F32), part_ref[0:1, 0:1]],
        payload_ref, terms_ref, idtail_ref, r,
    )


def untouched_kernel(xors, me_ref, w_ref, *refs):
    tails, out_ref = refs[:-1], refs[-1]
    per, width = w_ref.shape
    mine = (iota((per, width), 0) + me_ref[0] * per).astype(F32)
    count = jnp.zeros((per, width), F32)
    for tail in tails:
        count = count + (mine == ids_of(tail[per : per + TAIL, :])).astype(F32)
    free = jnp.sum(count, axis=1, keepdims=True) == 0.0
    w = w_ref[...]
    out_ref[...] = jnp.broadcast_to(total(jnp.where(free, w * w, 0.0)), out_ref.shape)


def sums_of(blocks):
    row = None
    for block in blocks:
        each = block.shape[0] // 2
        for at in (each, 2 * each):
            tail = block[at - TAIL : at, :].astype(F32)
            part = tail[2:3] + tail[3:4] + tail[4:5]
            row = part if row is None else row + part
    return row


def step_scalars(first, row, state):
    delta, zaz, zs = lane(row, 0), lane(row, 1), lane(row, 2)
    if first:
        free = lane(row, 3)
        rho = sigma = jnp.ones((1, 1), F32)
        delta, zaz = delta + free, zaz + free
        beta = jnp.zeros((1, 1), F32)
        pap = zaz
    else:
        delta_old, pap_old, rho, sigma, free = (lane(state, at) for at in range(5))
        delta, zaz, zs = delta + rho * rho * free, zaz + rho * rho * free, zs + rho * sigma * free
        beta = delta / delta_old
        pap = zaz + 2.0 * beta * zs + beta * beta * pap_old
        sigma = rho + beta * sigma
    alpha = delta / pap
    rho = rho - alpha * sigma
    return delta, pap, rho, sigma, free, alpha, beta


def pack_row(scalars, shape):
    out = jnp.zeros(shape, F32)
    for at, value in enumerate(scalars):
        out = jnp.where(iota(shape, 1) == at, value, out)
    return out


def step_kernel(first, n, *refs):
    blocks = refs[:n]
    ccol_ref, idtail_ref, curv_ref, weight_ref, m_ref, r_in, z_in, s_in, state_in = refs[n : n + 9]
    terms_in, sent_in, owed_in, tiles_hbm = refs[n + 9 : n + 13]
    payload_ref, r_ref, z_ref, s_ref, state_ref, terms_ref, sent_ref, owed_ref = refs[n + 13 : n + 21]
    tiles, zrows, terms, sems = refs[n + 21 :]
    copies = start_tiles(tiles_hbm, tiles, sems)
    ccol = ccol_ref[...]
    slots, width = ccol.shape
    each = slots + TAIL
    scalars = step_scalars(first, sums_of(blocks), state_in[0:1, :])
    alpha, beta = scalars[5:7]
    state_ref[...] = pack_row(scalars, state_ref.shape)
    image = z_in[...]
    for block in blocks:
        for at in range(0, block.shape[0], each):
            hot = hot_of(ccol, block, at + slots).astype(BF16)
            image = image + jnp.dot(hot, block[at : at + slots, :], preferred_element_type=F32)
    s = image if first else image + beta * s_in[...]
    r = r_in[...] - alpha * s
    z = r / m_ref[...]
    s_ref[...] = s
    r_ref[...] = r
    z_ref[...] = z
    sent = terms_in[...] if first else terms_in[...] + beta * sent_in[...]
    owed = owed_in[...] + alpha * sent
    sent_ref[...] = sent
    owed_ref[...] = owed
    if payload_ref.shape[0] > each:
        payload_ref[slots : 2 * slots, :] = owed.astype(BF16)
    weight = weight_ref[...]
    apply_and_pack(
        copies, tiles, ccol, z, zrows, terms, curv_ref, weight, [total(weight * z * s)], payload_ref, terms_ref,
        idtail_ref, r,
    )


def last_kernel(n, iters, me_ref, w_ref, state_a, state_b, *refs):
    lists = [refs[i * n : (i + 1) * n] for i in range(iters + 1)]
    newton_ref, residual_ref, stack, hots = refs[(iters + 1) * n :]
    per, width = w_ref.shape
    first_each = lists[0][0].shape[0] // 2
    slots = (first_each - TAIL) // 2
    mine = (iota((per, width), 0) + me_ref[0] * per).astype(F32)
    row = 0
    for index in range(n):
        for half in range(2):
            at = half * first_each
            block = lists[0][index]
            hots[:, row : row + slots] = hot_of(mine, block, at + 2 * slots).astype(BF16)
            stack[row : row + slots, 0:width] = block[at : at + slots, :]
            stack[row : row + slots, width : 2 * width] = block[at + slots : at + 2 * slots, :]
            for it in range(iters):
                low = half * (lists[1 + it][index].shape[0] // 2)
                stack[row : row + slots, (2 + it) * width : (3 + it) * width] = lists[1 + it][index][low : low + slots, :]
            stack[row : row + slots, (2 + iters) * width :] = lists[iters][index][low + slots : low + 2 * slots, :]
            row += slots
    state_c = pack_row(step_scalars(False, sums_of(lists[iters]), state_b[0:1, :]), (1, width))
    states = [state_a[0:1, :], state_b[0:1, :], state_c]
    for low in range(0, per, width):
        sums = jnp.dot(hots[low : low + width, :], stack[...], preferred_element_type=F32)
        g, d = sums[:, 0:width], sums[:, width : 2 * width]
        w = w_ref[low : low + width, :]
        m = d + RIDGE
        r = -(g + RIDGE * w)
        x = jnp.zeros_like(r)
        p = s = None
        for it in range(iters):
            alpha, beta = lane(states[it], 5), lane(states[it], 6)
            z = r / m
            image = sums[:, (2 + it) * width : (3 + it) * width] + RIDGE * z
            p = z if it == 0 else z + beta * p
            s = image if it == 0 else image + beta * s
            if it == iters - 1:
                r = -(sums[:, (2 + iters) * width :] + RIDGE * w) - RIDGE * x
            x = x + alpha * p
            r = r - alpha * s
        newton_ref[low : low + width, :] = x
        residual_ref[low : low + width, :] = r


def local(tiles, column_blocks, occupied, labels, weights):
    me = lax.axis_index("ex").astype(jnp.int32).reshape(1)
    per, width = weights.shape
    r_all, k_all = tiles.shape[:2]
    slots = r_all * k_all
    n_dev = lax.axis_size("ex")
    smem = pl.BlockSpec(memory_space=pltpu.SMEM)
    sds = jax.ShapeDtypeStruct
    square = sds((slots, width), F32)

    payload, ccol, idtail = pl.pallas_call(
        prep_kernel,
        out_shape=(sds((per + TAIL, width), BF16), square, sds((TAIL, width), F32)),
        in_specs=[VMEM] * 3,
        out_specs=(VMEM,) * 3,
        compiler_params=params(),
        name="prep",
    )(column_blocks, occupied, weights)

    wide = gather_wide(payload)
    xors, wide = [xor for xor, _ in wide], [block for _, block in wide]
    tile_scratch = pltpu.VMEM(tiles.shape, BF16)
    sems = pltpu.SemaphoreType.DMA((r_all,))
    cell = pltpu.VMEM((slots, width), F32)

    payload, wslot, curv, grad = pl.pallas_call(
        functools.partial(first_kernel, xors),
        out_shape=(sds((2 * slots + TAIL, width), BF16), square, sds((r_all, width, width), F32), square),
        in_specs=[smem] + [VMEM] * (len(wide) + 3) + [ANY],
        out_specs=(VMEM,) * 4,
        scratch_shapes=[tile_scratch, cell, cell, sems],
        compiler_params=params(),
        name="margins",
    )(me, *wide, ccol, idtail, labels, tiles)

    part = pl.pallas_call(
        functools.partial(untouched_kernel, xors),
        out_shape=sds((8, width), F32),
        in_specs=[smem] + [VMEM] * (len(wide) + 1),
        out_specs=VMEM,
        compiler_params=params(),
        name="untouched",
    )(me, weights, *wide)

    exchanged = [gather_blocks(payload)]
    n = len(exchanged[0])
    payload_shape = sds((slots + TAIL, width), BF16)
    scratch = [tile_scratch, cell, cell, sems]
    payload, m, r, z, weight, terms = pl.pallas_call(
        functools.partial(start_kernel, n),
        out_shape=(payload_shape, square, square, square, square, square),
        in_specs=[VMEM] * (n + 5) + [ANY],
        out_specs=(VMEM,) * 6,
        scratch_shapes=scratch,
        compiler_params=params(),
        name="start",
    )(*exchanged[0], ccol, idtail, wslot, curv, part, tiles)

    iters = 3
    states, s, state, sent, owed = [], z, part, terms, grad
    for it in range(iters - 1):
        exchanged.append(gather_blocks(payload))
        shape = payload_shape if it < iters - 2 else sds((2 * slots + TAIL, width), BF16)
        payload, r, z, s, state, terms, sent, owed = pl.pallas_call(
            functools.partial(step_kernel, it == 0, n),
            out_shape=(shape, square, square, square, sds((8, width), F32), square, square, square),
            in_specs=[VMEM] * (n + 12) + [ANY],
            out_specs=(VMEM,) * 8,
            scratch_shapes=scratch,
            compiler_params=params(),
            name=f"step_{it}",
        )(*exchanged[-1], ccol, idtail, curv, weight, m, r, z, s, state, terms, sent, owed, tiles)
        states.append(state)
    exchanged.append(gather_blocks(payload))

    flat = [block for blocks in exchanged for block in blocks]
    return pl.pallas_call(
        functools.partial(last_kernel, n, iters),
        out_shape=(sds(weights.shape, F32), sds(weights.shape, F32)),
        in_specs=[smem] + [VMEM] * (3 + len(flat)),
        out_specs=(VMEM, VMEM),
        scratch_shapes=[
            pltpu.VMEM((n_dev * slots, (3 + iters) * width), BF16),
            pltpu.VMEM((per, n_dev * slots), BF16),
        ],
        compiler_params=params(),
        name="finish",
    )(me, weights, *states, *flat)


def solution(mesh):
    placed = (
        P(("groups", "ex"), None, None, None),
        P(("groups", "ex"), None),
        P(("groups", "ex"), None),
        P(("groups", "ex"), None),
        P(("groups", "ex"), None),
    )
    return jax.shard_map(
        local,
        mesh=mesh,
        in_specs=placed,
        out_specs=(P(("groups", "ex"), None), P(("groups", "ex"), None)),
        check_vma=False,
    )
```

time: 754 us -> 116 us (0.15)
  waiting for transfers between devices: 520 us -> 43.4 us
  blocking collectives: 152 us -> 0 us
  starting transfers between devices: 0.55 us -> 46.9 us
  other arithmetic: 31.9 us -> 0 us
  Pallas kernels: 0 us -> 19.6 us
  between operations: 20.4 us -> 0.8 us
  matrix products: 17.4 us -> 0 us
    reduce_scatter x5 -> x0, waiting for transfers between devices: 358 us -> none  [the longest x3 214 us: local(): image = lax.psum_scatter(dense_part, 'ex', scatter_dimension=0, tiled=True)]
    all_gather x4 -> x0, waiting for transfers between devices: 162 us -> none  [the longest x3 119 us: local(): lax.all_gather(direction.astype(jnp.bfloat16), 'ex', axis=0, tiled=True)]
    psum x5 -> x0, blocking collectives: 152 us -> none  [the longest x2 61.4 us: local(): curvature = lax.psum(jnp.sum(direction * image), 'ex')]
    ppermute x0 -> x47, starting transfers between devices: none -> 46.9 us  [swap(): lax.ppermute(x, 'ex', [(i, i ^ (second if i % 2 else first)) for i in ran...]
    ppermute x0 -> x47, waiting for transfers between devices: none -> 43.4 us  [swap(): lax.ppermute(x, 'ex', [(i, i ^ (second if i % 2 else first)) for i in ran...]
    pallas_call x0 -> x7, Pallas kernels: none -> 19.6 us  [the longest x2 7.14 us: local(): pl.pallas_call(functools.partial(step_kernel, it == 0, n), out_shape=(sha...]
    dot_general x9 -> x0, matrix products: 17.4 us -> none  [the longest x4 14.1 us: apply_picked(): jnp.einsum('bkij,bkj->bi', tiles, picked, preferred_element_type=jnp.floa...]
    scatter-add x5 -> x0, other arithmetic: 15.8 us -> none  [the longest x3 9.46 us: local(): jax.ops.segment_sum(terms, flat_blocks, num_segments=all_blocks)]
  transfers between devices with their start and end apart: 9 -> 47, of which waited for: 9 -> 22; matrix products, arithmetic and copies ran while one was open for 1% -> 0% of each run, Pallas kernels for 0% -> 1%
where the time goes in v1:
time: 116 us
  starting transfers between devices  46.9 us (40%)
  waiting for transfers between devices  43.4 us (37%)
  Pallas kernels  19.6 us (17%)
  local copies, waits for them, and re-layouts  5.25 us (5%)
    ppermute x47, starting transfers between devices, swap(): lax.ppermute(x, 'ex', [(i, i ^ (second if i % 2 else first)) for i in ran...  46.9 us
    ppermute x47, waiting for transfers between devices, swap(): lax.ppermute(x, 'ex', [(i, i ^ (second if i % 2 else first)) for i in ran...  43.4 us
    pallas_call x2, Pallas kernels, local(): pl.pallas_call(functools.partial(step_kernel, it == 0, n), out_shape=(sha...  7.14 us
    unnamed x18, local copies, waits for them, and re-layouts  5.2 us
    pallas_call x1, Pallas kernels, local(): pl.pallas_call(functools.partial(first_kernel, xors), out_shape=(sds((2 *...  5.05 us
    pallas_call x1, Pallas kernels, local(): pl.pallas_call(functools.partial(start_kernel, n), out_shape=(payload_sha...  3.34 us
    pallas_call x1, Pallas kernels, local(): pl.pallas_call(functools.partial(last_kernel, n, iters), out_shape=(sds(w...  3.32 us
  transfers between devices with their start and end apart: 47, of which 22 were waited for; matrix products, arithmetic and copies ran while one was open for 0% of the time, Pallas kernels for 1%

profile of v1, /device:TPU:0, one launch (start us, length us, event | category | flops | bytes accessed | tf_op | source)
XLA Modules:
  0.0 115.9 jit_solution(12720944557321177173)
XLA Ops:
  0.6 0.9 copy-done.2
  1.6 0.7 copy-done.4
  2.3 0.7 copy-done.5
  2.9 0.2 prep.1
  3.1 5.1 %collective-permute-start.3 = (bf16[528,128]{1,0:T(8,128)(2,1)S(1)}, bf16[528,128]{1,0:T(8,128)(2,1)S(1)}, u32[]{:S(2)}, u32[]{:S(2)}) collective-permute-start(bf16[528,128]{1,0:T(8,128)(2,1)S(1)} %get-tuple-element.25.refs_0_), channel_id=1, source_target_pairs={{0,12},{1,13},{2,14},{3,15},{4,8},{5,9},{6,10},{7,11},{8,4},{9,5},... | collective-permute-start | bytes 405512 | tf_op jit(solution)/shard_map/ppermute | solution.py:30
  8.2 0.7 collective-permute-start.1
  9.0 1.6 %collective-permute-start = (bf16[528,128]{1,0:T(8,128)(2,1)S(1)}, bf16[528,128]{1,0:T(8,128)(2,1)S(1)}, u32[]{:S(2)}, u32[]{:S(2)}) collective-permute-start(bf16[528,128]{1,0:T(8,128)(2,1)S(1)} %get-tuple-element.25.refs_0_), channel_id=1, source_target_pairs={{0,2},{1,3},{2,0},{3,1},{4,6},{5,7},{6,4},{7,5},{8,10},{9,11},{10,... | collective-permute-start | bytes 405512 | tf_op jit(solution)/shard_map/ppermute | solution.py:30
  10.5 2.0 %collective-permute-done.3.refs_4_ = bf16[528,128]{1,0:T(8,128)(2,1)S(1)} collective-permute-done((bf16[528,128]{1,0:T(8,128)(2,1)S(1)}, bf16[528,128]{1,0:T(8,128)(2,1)S(1)}, u32[]{:S(2)}, u32[]{:S(2)}) %collective-permute-start.3) | collective-permute-done | bytes 135200 | tf_op jit(solution)/shard_map/ppermute | solution.py:30
  12.5 1.6 %collective-permute-start.6 = (bf16[528,128]{1,0:T(8,128)(2,1)S(1)}, bf16[528,128]{1,0:T(8,128)(2,1)S(1)}, u32[]{:S(2)}, u32[]{:S(2)}) collective-permute-start(bf16[528,128]{1,0:T(8,128)(2,1)S(1)} %collective-permute-done.3.refs_4_), channel_id=1, source_target_pairs={{0,2},{1,3},{2,0},{3,1},{4,6},{5,7},{6,4},{7,5},{8,10},{9,11},{10,... | collective-permute-start | bytes 405512 | tf_op jit(solution)/shard_map/ppermute | solution.py:30
  14.1 5.6 %collective-permute-done.2.refs_3_ = bf16[528,128]{1,0:T(8,128)(2,1)S(1)} collective-permute-done((bf16[528,128]{1,0:T(8,128)(2,1)S(1)}, bf16[528,128]{1,0:T(8,128)(2,1)S(1)}, u32[]{:S(2)}, u32[]{:S(2)}) %collective-permute-start.2) | collective-permute-done | bytes 135200 | tf_op jit(solution)/shard_map/ppermute | solution.py:30
  19.7 1.5 %collective-permute-start.5 = (bf16[528,128]{1,0:T(8,128)(2,1)S(1)}, bf16[528,128]{1,0:T(8,128)(2,1)S(1)}, u32[]{:S(2)}, u32[]{:S(2)}) collective-permute-start(bf16[528,128]{1,0:T(8,128)(2,1)S(1)} %collective-permute-done.2.refs_3_), channel_id=1, source_target_pairs={{0,2},{1,3},{2,0},{3,1},{4,6},{5,7},{6,4},{7,5},{8,10},{9,11},{10,... | collective-permute-start | bytes 405512 | tf_op jit(solution)/shard_map/ppermute | solution.py:30
  21.2 0.5 collective-permute-start.4
  21.7 0.5 collective-permute-start.8
  22.3 3.8 %collective-permute-done.5.refs_6_ = bf16[528,128]{1,0:T(8,128)(2,1)S(1)} collective-permute-done((bf16[528,128]{1,0:T(8,128)(2,1)S(1)}, bf16[528,128]{1,0:T(8,128)(2,1)S(1)}, u32[]{:S(2)}, u32[]{:S(2)}) %collective-permute-start.5) | collective-permute-done | bytes 135200 | tf_op jit(solution)/shard_map/ppermute | solution.py:30
  26.1 2.5 %collective-permute-done.4.refs_5_ = bf16[528,128]{1,0:T(8,128)(2,1)S(1)} collective-permute-done((bf16[528,128]{1,0:T(8,128)(2,1)S(1)}, bf16[528,128]{1,0:T(8,128)(2,1)S(1)}, u32[]{:S(2)}, u32[]{:S(2)}) %collective-permute-start.4) | collective-permute-done | bytes 135200 | tf_op jit(solution)/shard_map/ppermute | solution.py:30
  28.6 1.3 %collective-permute-done.12.refs_13_ = bf16[528,128]{1,0:T(8,128)(2,1)S(1)} collective-permute-done((bf16[528,128]{1,0:T(8,128)(2,1)S(1)}, bf16[528,128]{1,0:T(8,128)(2,1)S(1)}, u32[]{:S(2)}, u32[]{:S(2)}) %collective-permute-start.12) | collective-permute-done | bytes 135200 | tf_op jit(solution)/shard_map/ppermute | solution.py:30
  29.9 2.2 %copy-done = bf16[4,32,128,128]{3,2,1,0:T(8,128)(2,1)S(1)} copy-done((bf16[4,32,128,128]{3,2,1,0:T(8,128)(2,1)S(1)}, bf16[4,32,128,128]{3,2,1,0:T(8,128)(2,1)}, u32[]{:S(2)}) %copy-start) | copy-done | bytes 4194328
  32.1 0.7 copy-done.6
  32.8 5.1 %margins.1 = (bf16[272,128]{1,0:T(8,128)(2,1)S(1)}, f32[128,128]{1,0:T(8,128)S(1)}, f32[4,128,128]{2,1,0:T(8,128)S(1)}, f32[128,128]{1,0:T(8,128)S(1)}) custom-call(s32[1]{0:T(128)} %bitcast.me_ref, bf16[528,128]{1,0:T(8,128)(2,1)S(1)} %get-tuple-element.25.refs_0_, bf16[528,128]{1,0:T(8,128)(2,1)S(1)} %collective-permute-done.refs_1_, ...), custom_call_target="tpu_custom_call" | custom-call | tf_op jit(solution)/shard_map/margins/pallas_call | solution.py:385
  37.8 0.2 collective-permute-start.15
  38.1 1.1 collective-permute-done.15
  39.2 3.6 %collective-permute-start.21 = (bf16[544,128]{1,0:T(8,128)(2,1)S(1)}, bf16[544,128]{1,0:T(8,128)(2,1)S(1)}, u32[]{:S(2)}, u32[]{:S(2)}) collective-permute-start(bf16[544,128]{1,0:T(8,128)(2,1)S(1)} %constant_dynamic-update-slice_fusion.refs_0_), channel_id=1, source_target_pairs={{0,10},{1,13},{2,8},{3,15},{4,14},{5,9},{6,12},{7,11},{8,2},{9,5},... | collective-permute-start | bytes 417800 | tf_op jit(solution)/shard_map/ppermute | solution.py:30
  42.8 0.4 collective-permute-start.19
  43.2 1.5 %collective-permute-start.17 = (bf16[544,128]{1,0:T(8,128)(2,1)S(1)}, bf16[544,128]{1,0:T(8,128)(2,1)S(1)}, u32[]{:S(2)}, u32[]{:S(2)}) collective-permute-start(bf16[544,128]{1,0:T(8,128)(2,1)S(1)} %constant_dynamic-update-slice_fusion.refs_0_), channel_id=1, source_target_pairs={{0,2},{1,5},{2,0},{3,7},{4,6},{5,1},{6,4},{7,3},{8,10},{9,13},{10,... | collective-permute-start | bytes 417800 | tf_op jit(solution)/shard_map/ppermute | solution.py:30
  44.7 1.3 %collective-permute-start.16 = (bf16[544,128]{1,0:T(8,128)(2,1)S(1)}, bf16[544,128]{1,0:T(8,128)(2,1)S(1)}, u32[]{:S(2)}, u32[]{:S(2)}) collective-permute-start(bf16[544,128]{1,0:T(8,128)(2,1)S(1)} %constant_dynamic-update-slice_fusion.refs_0_), channel_id=1, source_target_pairs={{0,14},{1,15},{2,12},{3,13},{4,10},{5,11},{6,8},{7,9},{8,6},{9,7},... | collective-permute-start | bytes 417800 | tf_op jit(solution)/shard_map/ppermute | solution.py:30
  46.0 6.5 %collective-permute-done.21.refs_6_ = bf16[544,128]{1,0:T(8,128)(2,1)S(1)} collective-permute-done((bf16[544,128]{1,0:T(8,128)(2,1)S(1)}, bf16[544,128]{1,0:T(8,128)(2,1)S(1)}, u32[]{:S(2)}, u32[]{:S(2)}) %collective-permute-start.21) | collective-permute-done | bytes 139296 | tf_op jit(solution)/shard_map/ppermute | solution.py:30
  52.5 2.7 %collective-permute-start.20 = (bf16[544,128]{1,0:T(8,128)(2,1)S(1)}, bf16[544,128]{1,0:T(8,128)(2,1)S(1)}, u32[]{:S(2)}, u32[]{:S(2)}) collective-permute-start(bf16[544,128]{1,0:T(8,128)(2,1)S(1)} %collective-permute-done.19.refs_4_), channel_id=1, source_target_pairs={{0,1},{1,0},{2,3},{3,2},{4,5},{5,4},{6,7},{7,6},{8,9},{9,8},{10,11... | collective-permute-start | bytes 417800 | tf_op jit(solution)/shard_map/ppermute | solution.py:30
  55.2 0.6 untouched.1.refs_12_.refs_16_
  55.8 0.4 collective-permute-done.20.refs_5_
  56.2 0.4 collective-permute-done.18.refs_3_
  56.6 3.3 %start.1 = (bf16[144,128]{1,0:T(8,128)(2,1)S(1)}, f32[128,128]{1,0:T(8,128)S(1)}, f32[128,128]{1,0:T(8,128)S(1)}, f32[128,128]{1,0:T(8,128)S(1)}, f32[128,128]{1,0:T(8,128)S(1)}, /*index=5*/f32[128,128]{1,0:T(8,128)S(1)}) custom-call(bf16[544,128]{1,0:T(8,128)(2,1)S(1)} %constant_dynamic-update-slice_fusion.refs_0_, ...), custom_call_target="tpu_custom_call" | custom-call | tf_op jit(solution)/shard_map/start/pallas_call | solution.py:408
  59.9 0.3 collective-permute-start.23
  60.2 1.0 collective-permute-done.23
  61.2 3.4 %collective-permute-start.29 = (bf16[288,128]{1,0:T(8,128)(2,1)S(1)}, bf16[288,128]{1,0:T(8,128)(2,1)S(1)}, u32[]{:S(2)}, u32[]{:S(2)}) collective-permute-start(bf16[288,128]{1,0:T(8,128)(2,1)S(1)} %constant_dynamic-update-slice_fusion.2.refs_0_.refs_8_), channel_id=1, source_target_pairs={{0,10},{1,13},{2,8},{3,15},{4,14},{5,9},{6,12},{7,11},{8,2},{9,5},... | collective-permute-start | bytes 221192 | tf_op jit(solution)/shard_map/ppermute | solution.py:30
  64.7 0.9 collective-permute-start.27
  65.5 1.7 %collective-permute-start.25 = (bf16[288,128]{1,0:T(8,128)(2,1)S(1)}, bf16[288,128]{1,0:T(8,128)(2,1)S(1)}, u32[]{:S(2)}, u32[]{:S(2)}) collective-permute-start(bf16[288,128]{1,0:T(8,128)(2,1)S(1)} %constant_dynamic-update-slice_fusion.2.refs_0_.refs_8_), channel_id=1, source_target_pairs={{0,2},{1,5},{2,0},{3,7},{4,6},{5,1},{6,4},{7,3},{8,10},{9,13},{10,... | collective-permute-start | bytes 221192 | tf_op jit(solution)/shard_map/ppermute | solution.py:30
  67.2 0.8 collective-permute-start.24
  68.0 1.9 %collective-permute-done.29.refs_6_.refs_14_ = bf16[288,128]{1,0:T(8,128)(2,1)S(1)} collective-permute-done((bf16[288,128]{1,0:T(8,128)(2,1)S(1)}, bf16[288,128]{1,0:T(8,128)(2,1)S(1)}, u32[]{:S(2)}, u32[]{:S(2)}) %collective-permute-start.29) | collective-permute-done | bytes 73760 | tf_op jit(solution)/shard_map/ppermute | solution.py:30
  69.9 0.1 collective-permute-done.27.refs_4_.refs_12_
  70.0 0.5 collective-permute-start.28
  70.5 0.2 collective-permute-done.25.refs_2_.refs_10_
  70.7 3.6 %collective-permute-done.24.refs_1_.refs_9_ = bf16[288,128]{1,0:T(8,128)(2,1)S(1)} collective-permute-done((bf16[288,128]{1,0:T(8,128)(2,1)S(1)}, bf16[288,128]{1,0:T(8,128)(2,1)S(1)}, u32[]{:S(2)}, u32[]{:S(2)}) %collective-permute-start.24) | collective-permute-done | bytes 73760 | tf_op jit(solution)/shard_map/ppermute | solution.py:30
  74.3 3.3 %step_0.1 = (bf16[144,128]{1,0:T(8,128)(2,1)S(1)}, f32[128,128]{1,0:T(8,128)S(1)}, f32[128,128]{1,0:T(8,128)S(1)}, f32[128,128]{1,0:T(8,128)S(1)}, f32[8,128]{1,...) custom-call(bf16[288,128]{1,0:T(8,128)(2,1)S(1)} %constant_dynamic-update-slice_fusion.2.refs, ...), custom_call_target="tpu_custom_call" | custom-call | tf_op jit(solution)/shard_map/step_0/pallas_call | solution.py:423
  77.6 1.2 %collective-permute-done.31 = bf16[144,128]{1,0:T(8,128)(2,1)S(1)} collective-permute-done((bf16[144,128]{1,0:T(8,128)(2,1)S(1)}, bf16[144,128]{1,0:T(8,128)(2,1)S(1)}, u32[]{:S(2)}, u32[]{:S(2)}) %collective-permute-start.31) | collective-permute-done | bytes 36896 | tf_op jit(solution)/shard_map/ppermute | solution.py:30
  78.8 2.2 %collective-permute-start.37 = (bf16[288,128]{1,0:T(8,128)(2,1)S(1)}, bf16[288,128]{1,0:T(8,128)(2,1)S(1)}, u32[]{:S(2)}, u32[]{:S(2)}) collective-permute-start(bf16[288,128]{1,0:T(8,128)(2,1)S(1)} %constant_dynamic-update-slice_fusion.4.refs_0_.refs_16_), channel_id=1, source_target_pairs={{0,10},{1,13},{2,8},{3,15},{4,14},{5,9},{6,12},{7,11},{8,2},{9,5},... | collective-permute-start | bytes 221192 | tf_op jit(solution)/shard_map/ppermute | solution.py:30
  81.1 0.5 collective-permute-start.35
  81.6 1.0 collective-permute-start.33
  82.6 3.1 %collective-permute-start.32 = (bf16[288,128]{1,0:T(8,128)(2,1)S(1)}, bf16[288,128]{1,0:T(8,128)(2,1)S(1)}, u32[]{:S(2)}, u32[]{:S(2)}) collective-permute-start(bf16[288,128]{1,0:T(8,128)(2,1)S(1)} %constant_dynamic-update-slice_fusion.4.refs_0_.refs_16_), channel_id=1, source_target_pairs={{0,14},{1,15},{2,12},{3,13},{4,10},{5,11},{6,8},{7,9},{8,6},{9,7},... | collective-permute-start | bytes 221192 | tf_op jit(solution)/shard_map/ppermute | solution.py:30
  85.7 2.0 %collective-permute-done.37.refs_6_.refs_22_ = bf16[288,128]{1,0:T(8,128)(2,1)S(1)} collective-permute-done((bf16[288,128]{1,0:T(8,128)(2,1)S(1)}, bf16[288,128]{1,0:T(8,128)(2,1)S(1)}, u32[]{:S(2)}, u32[]{:S(2)}) %collective-permute-start.37) | collective-permute-done | bytes 73760 | tf_op jit(solution)/shard_map/ppermute | solution.py:30
  87.6 0.2 collective-permute-done.35.refs_4_.refs_20_
  87.8 0.3 collective-permute-start.36
  88.2 0.2 collective-permute-start.34
  88.3 1.3 %collective-permute-done.32.refs_1_.refs_17_ = bf16[288,128]{1,0:T(8,128)(2,1)S(1)} collective-permute-done((bf16[288,128]{1,0:T(8,128)(2,1)S(1)}, bf16[288,128]{1,0:T(8,128)(2,1)S(1)}, u32[]{:S(2)}, u32[]{:S(2)}) %collective-permute-start.32) | collective-permute-done | bytes 73760 | tf_op jit(solution)/shard_map/ppermute | solution.py:30
  89.6 3.9 %step_1.1 = (bf16[272,128]{1,0:T(8,128)(2,1)S(1)}, f32[128,128]{1,0:T(8,128)}, f32[128,128]{1,0:T(8,128)}, f32[128,128]{1,0:T(8,128)}, f32[8,128]{1,0:T(8,128)S(...) custom-call(bf16[288,128]{1,0:T(8,128)(2,1)S(1)} %constant_dynamic-update-slice_fusion.4.refs_0_.refs_16_, ...), custom_call_target="tpu_custom_call" | custom-call | tf_op jit(solution)/shard_map/step_1/pallas_call | solution.py:423
  93.6 1.2 %collective-permute-done.39 = bf16[272,128]{1,0:T(8,128)(2,1)S(1)} collective-permute-done((bf16[272,128]{1,0:T(8,128)(2,1)S(1)}, bf16[272,128]{1,0:T(8,128)(2,1)S(1)}, u32[]{:S(2)}, u32[]{:S(2)}) %collective-permute-start.39) | collective-permute-done | bytes 69664 | tf_op jit(solution)/shard_map/ppermute | solution.py:30
  94.8 1.5 %collective-permute-start.45 = (bf16[544,128]{1,0:T(8,128)(2,1)S(1)}, bf16[544,128]{1,0:T(8,128)(2,1)S(1)}, u32[]{:S(2)}, u32[]{:S(2)}) collective-permute-start(bf16[544,128]{1,0:T(8,128)(2,1)S(1)} %constant_dynamic-update-slice_fusion.6.refs_24_), channel_id=1, source_target_pairs={{0,10},{1,13},{2,8},{3,15},{4,14},{5,9},{6,12},{7,11},{8,2},{9,5},... | collective-permute-start | bytes 417800 | tf_op jit(solution)/shard_map/ppermute | solution.py:30
  96.3 2.3 %collective-permute-start.43 = (bf16[544,128]{1,0:T(8,128)(2,1)S(1)}, bf16[544,128]{1,0:T(8,128)(2,1)S(1)}, u32[]{:S(2)}, u32[]{:S(2)}) collective-permute-start(bf16[544,128]{1,0:T(8,128)(2,1)S(1)} %constant_dynamic-update-slice_fusion.6.refs_24_), channel_id=1, source_target_pairs={{0,6},{1,9},{2,4},{3,11},{4,2},{5,13},{6,0},{7,15},{8,14},{9,1},{1... | collective-permute-start | bytes 417800 | tf_op jit(solution)/shard_map/ppermute | solution.py:30
  98.6 1.4 %collective-permute-start.41 = (bf16[544,128]{1,0:T(8,128)(2,1)S(1)}, bf16[544,128]{1,0:T(8,128)(2,1)S(1)}, u32[]{:S(2)}, u32[]{:S(2)}) collective-permute-start(bf16[544,128]{1,0:T(8,128)(2,1)S(1)} %constant_dynamic-update-slice_fusion.6.refs_24_), channel_id=1, source_target_pairs={{0,2},{1,5},{2,0},{3,7},{4,6},{5,1},{6,4},{7,3},{8,10},{9,13},{10,... | collective-permute-start | bytes 417800 | tf_op jit(solution)/shard_map/ppermute | solution.py:30
  100.0 1.6 %collective-permute-start.40 = (bf16[544,128]{1,0:T(8,128)(2,1)S(1)}, bf16[544,128]{1,0:T(8,128)(2,1)S(1)}, u32[]{:S(2)}, u32[]{:S(2)}) collective-permute-start(bf16[544,128]{1,0:T(8,128)(2,1)S(1)} %constant_dynamic-update-slice_fusion.6.refs_24_), channel_id=1, source_target_pairs={{0,14},{1,15},{2,12},{3,13},{4,10},{5,11},{6,8},{7,9},{8,6},{9,7},... | collective-permute-start | bytes 417800 | tf_op jit(solution)/shard_map/ppermute | solution.py:30
  101.7 5.9 %collective-permute-done.45.refs_30_ = bf16[544,128]{1,0:T(8,128)(2,1)S(1)} collective-permute-done((bf16[544,128]{1,0:T(8,128)(2,1)S(1)}, bf16[544,128]{1,0:T(8,128)(2,1)S(1)}, u32[]{:S(2)}, u32[]{:S(2)}) %collective-permute-start.45) | collective-permute-done | bytes 139296 | tf_op jit(solution)/shard_map/ppermute | solution.py:30
  107.5 3.7 %collective-permute-start.44 = (bf16[544,128]{1,0:T(8,128)(2,1)S(1)}, bf16[544,128]{1,0:T(8,128)(2,1)S(1)}, u32[]{:S(2)}, u32[]{:S(2)}) collective-permute-start(bf16[544,128]{1,0:T(8,128)(2,1)S(1)} %collective-permute-done.43.refs_28_), channel_id=1, source_target_pairs={{0,1},{1,0},{2,3},{3,2},{4,5},{5,4},{6,7},{7,6},{8,9},{9,8},{10,11... | collective-permute-start | bytes 417800 | tf_op jit(solution)/shard_map/ppermute | solution.py:30
  111.3 1.0 collective-permute-done.44.refs_29_
  112.2 0.4 collective-permute-done.42.refs_27_
  112.6 3.3 %finish.1 = (f32[512,128]{1,0:T(8,128)}, f32[512,128]{1,0:T(8,128)}) custom-call(s32[1]{0:T(128)} %bitcast.me_ref, f32[512,128]{1,0:T(8,128)S(1)} %copy-done.3, f32[8,128]{1,0:T(8,128)S(1)} %get-tuple-element.38.refs_16_.state_a, f32[8,128]{1,0:T(8,128)S(1)} %get-tuple-element.46.state_b, bf16[544,128]{1,0:T(8,128)(2,1)S(1)} %constant_dynamic-update-slice_fusion.refs_0_, ...), custom_call_target="tpu_custom_call" | custom-call | tf_op jit(solution)/shard_map/finish/pallas_call | solution.py:436
  (59 shorter events, 0.4 us)
Async XLA Ops:
  0.6 1.0 copy-start.2
  1.6 0.7 copy-start.4
  2.3 0.7 copy-start.5
  2.9 52.3 %copy-start.3 = (f32[512,128]{1,0:T(8,128)S(1)}, f32[512,128]{1,0:T(8,128)}, u32[]{:S(2)}) copy-start(f32[512,128]{1,0:T(8,128)} %w_ref.5) | copy-start | bytes 786436
  3.1 9.4 %collective-permute-start.3 = (bf16[528,128]{1,0:T(8,128)(2,1)S(1)}, bf16[528,128]{1,0:T(8,128)(2,1)S(1)}, u32[]{:S(2)}, u32[]{:S(2)}) collective-permute-start(bf16[528,128]{1,0:T(8,128)(2,1)S(1)} %get-tuple-element.25.refs_0_), channel_id=1, source_target_pairs={{0,12},{1,13},{2,14},{3,15},{4,8},{5,9},{6,10},{7,11},{8,4},{9,5},... | collective-permute-start | bytes 405512 | tf_op jit(solution)/shard_map/ppermute | solution.py:30
  8.2 4.3 %collective-permute-start.7 = (bf16[528,128]{1,0:T(8,128)(2,1)S(1)}, bf16[528,128]{1,0:T(8,128)(2,1)S(1)}, u32[]{:S(2)}, u32[]{:S(2)}) collective-permute-start(bf16[528,128]{1,0:T(8,128)(2,1)S(1)} %get-tuple-element.25.refs_0_), channel_id=1, source_target_pairs={{0,1},{1,0},{2,3},{3,2},{4,5},{5,4},{6,7},{7,6},{8,9},{9,8},{10,11... | collective-permute-start | bytes 405512 | tf_op jit(solution)/shard_map/ppermute | solution.py:30
  8.2 11.4 %collective-permute-start.2 = (bf16[528,128]{1,0:T(8,128)(2,1)S(1)}, bf16[528,128]{1,0:T(8,128)(2,1)S(1)}, u32[]{:S(2)}, u32[]{:S(2)}) collective-permute-start(bf16[528,128]{1,0:T(8,128)(2,1)S(1)} %get-tuple-element.25.refs_0_), channel_id=1, source_target_pairs={{0,8},{1,9},{2,10},{3,11},{4,12},{5,13},{6,14},{7,15},{8,0},{9,1},... | collective-permute-start | bytes 405512 | tf_op jit(solution)/shard_map/ppermute | solution.py:30
  8.2 11.4 %collective-permute-start.1 = (bf16[528,128]{1,0:T(8,128)(2,1)S(1)}, bf16[528,128]{1,0:T(8,128)(2,1)S(1)}, u32[]{:S(2)}, u32[]{:S(2)}) collective-permute-start(bf16[528,128]{1,0:T(8,128)(2,1)S(1)} %get-tuple-element.25.refs_0_), channel_id=1, source_target_pairs={{0,4},{1,5},{2,6},{3,7},{4,0},{5,1},{6,2},{7,3},{8,12},{9,13},{10,... | collective-permute-start | bytes 405512 | tf_op jit(solution)/shard_map/ppermute | solution.py:30
  9.0 12.2 %collective-permute-start = (bf16[528,128]{1,0:T(8,128)(2,1)S(1)}, bf16[528,128]{1,0:T(8,128)(2,1)S(1)}, u32[]{:S(2)}, u32[]{:S(2)}) collective-permute-start(bf16[528,128]{1,0:T(8,128)(2,1)S(1)} %get-tuple-element.25.refs_0_), channel_id=1, source_target_pairs={{0,2},{1,3},{2,0},{3,1},{4,6},{5,7},{6,4},{7,5},{8,10},{9,11},{10,... | collective-permute-start | bytes 405512 | tf_op jit(solution)/shard_map/ppermute | solution.py:30
  12.5 9.2 %collective-permute-start.11 = (bf16[528,128]{1,0:T(8,128)(2,1)S(1)}, bf16[528,128]{1,0:T(8,128)(2,1)S(1)}, u32[]{:S(2)}, u32[]{:S(2)}) collective-permute-start(bf16[528,128]{1,0:T(8,128)(2,1)S(1)} %collective-permute-done.3.refs_4_), channel_id=1, source_target_pairs={{0,1},{1,0},{2,3},{3,2},{4,5},{5,4},{6,7},{7,6},{8,9},{9,8},{10,11... | collective-permute-start | bytes 405512 | tf_op jit(solution)/shard_map/ppermute | solution.py:30
  12.5 9.2 %collective-permute-start.6 = (bf16[528,128]{1,0:T(8,128)(2,1)S(1)}, bf16[528,128]{1,0:T(8,128)(2,1)S(1)}, u32[]{:S(2)}, u32[]{:S(2)}) collective-permute-start(bf16[528,128]{1,0:T(8,128)(2,1)S(1)} %collective-permute-done.3.refs_4_), channel_id=1, source_target_pairs={{0,2},{1,3},{2,0},{3,1},{4,6},{5,7},{6,4},{7,5},{8,10},{9,11},{10,... | collective-permute-start | bytes 405512 | tf_op jit(solution)/shard_map/ppermute | solution.py:30
  19.7 2.6 %collective-permute-start.10 = (bf16[528,128]{1,0:T(8,128)(2,1)S(1)}, bf16[528,128]{1,0:T(8,128)(2,1)S(1)}, u32[]{:S(2)}, u32[]{:S(2)}) collective-permute-start(bf16[528,128]{1,0:T(8,128)(2,1)S(1)} %collective-permute-done.2.refs_3_), channel_id=1, source_target_pairs={{0,1},{1,0},{2,3},{3,2},{4,5},{5,4},{6,7},{7,6},{8,9},{9,8},{10,11... | collective-permute-start | bytes 405512 | tf_op jit(solution)/shard_map/ppermute | solution.py:30
  19.7 6.4 %collective-permute-start.5 = (bf16[528,128]{1,0:T(8,128)(2,1)S(1)}, bf16[528,128]{1,0:T(8,128)(2,1)S(1)}, u32[]{:S(2)}, u32[]{:S(2)}) collective-permute-start(bf16[528,128]{1,0:T(8,128)(2,1)S(1)} %collective-permute-done.2.refs_3_), channel_id=1, source_target_pairs={{0,2},{1,3},{2,0},{3,1},{4,6},{5,7},{6,4},{7,5},{8,10},{9,11},{10,... | collective-permute-start | bytes 405512 | tf_op jit(solution)/shard_map/ppermute | solution.py:30
  21.2 7.4 %collective-permute-start.4 = (bf16[528,128]{1,0:T(8,128)(2,1)S(1)}, bf16[528,128]{1,0:T(8,128)(2,1)S(1)}, u32[]{:S(2)}, u32[]{:S(2)}) collective-permute-start(bf16[528,128]{1,0:T(8,128)(2,1)S(1)} %collective-permute-done.1.refs_2_), channel_id=1, source_target_pairs={{0,2},{1,3},{2,0},{3,1},{4,6},{5,7},{6,4},{7,5},{8,10},{9,11},{10,... | collective-permute-start | bytes 405512 | tf_op jit(solution)/shard_map/ppermute | solution.py:30
  21.7 6.9 %collective-permute-start.9 = (bf16[528,128]{1,0:T(8,128)(2,1)S(1)}, bf16[528,128]{1,0:T(8,128)(2,1)S(1)}, u32[]{:S(2)}, u32[]{:S(2)}) collective-permute-start(bf16[528,128]{1,0:T(8,128)(2,1)S(1)} %collective-permute-done.1.refs_2_), channel_id=1, source_target_pairs={{0,1},{1,0},{2,3},{3,2},{4,5},{5,4},{6,7},{7,6},{8,9},{9,8},{10,11... | collective-permute-start | bytes 405512 | tf_op jit(solution)/shard_map/ppermute | solution.py:30
  21.7 6.9 %collective-permute-start.8 = (bf16[528,128]{1,0:T(8,128)(2,1)S(1)}, bf16[528,128]{1,0:T(8,128)(2,1)S(1)}, u32[]{:S(2)}, u32[]{:S(2)}) collective-permute-start(bf16[528,128]{1,0:T(8,128)(2,1)S(1)} %collective-permute-done.refs_1_), channel_id=1, source_target_pairs={{0,1},{1,0},{2,3},{3,2},{4,5},{5,4},{6,7},{7,6},{8,9},{9,8},{10,11... | collective-permute-start | bytes 405512 | tf_op jit(solution)/shard_map/ppermute | solution.py:30
  22.2 6.4 %collective-permute-start.14 = (bf16[528,128]{1,0:T(8,128)(2,1)S(1)}, bf16[528,128]{1,0:T(8,128)(2,1)S(1)}, u32[]{:S(2)}, u32[]{:S(2)}) collective-permute-start(bf16[528,128]{1,0:T(8,128)(2,1)S(1)} %collective-permute-done.6.refs_7_), channel_id=1, source_target_pairs={{0,1},{1,0},{2,3},{3,2},{4,5},{5,4},{6,7},{7,6},{8,9},{9,8},{10,11... | collective-permute-start | bytes 405512 | tf_op jit(solution)/shard_map/ppermute | solution.py:30
  26.0 2.5 %collective-permute-start.13 = (bf16[528,128]{1,0:T(8,128)(2,1)S(1)}, bf16[528,128]{1,0:T(8,128)(2,1)S(1)}, u32[]{:S(2)}, u32[]{:S(2)}) collective-permute-start(bf16[528,128]{1,0:T(8,128)(2,1)S(1)} %collective-permute-done.5.refs_6_), channel_id=1, source_target_pairs={{0,1},{1,0},{2,3},{3,2},{4,5},{5,4},{6,7},{7,6},{8,9},{9,8},{10,11... | collective-permute-start | bytes 405512 | tf_op jit(solution)/shard_map/ppermute | solution.py:30
  28.6 1.4 %collective-permute-start.12 = (bf16[528,128]{1,0:T(8,128)(2,1)S(1)}, bf16[528,128]{1,0:T(8,128)(2,1)S(1)}, u32[]{:S(2)}, u32[]{:S(2)}) collective-permute-start(bf16[528,128]{1,0:T(8,128)(2,1)S(1)} %collective-permute-done.4.refs_5_), channel_id=1, source_target_pairs={{0,1},{1,0},{2,3},{3,2},{4,5},{5,4},{6,7},{7,6},{8,9},{9,8},{10,11... | collective-permute-start | bytes 405512 | tf_op jit(solution)/shard_map/ppermute | solution.py:30
  29.9 2.2 %copy-start = (bf16[4,32,128,128]{3,2,1,0:T(8,128)(2,1)S(1)}, bf16[4,32,128,128]{3,2,1,0:T(8,128)(2,1)}, u32[]{:S(2)}) copy-start(bf16[4,32,128,128]{3,2,1,0:T(8,128)(2,1)} %refs_20_.3) | copy-start | bytes 12582916
  32.1 0.7 copy-start.6
  32.8 23.8 %copy-start.1 = (bf16[4,32,128,128]{3,2,1,0:T(8,128)(2,1)S(1)}, bf16[4,32,128,128]{3,2,1,0:T(8,128)(2,1)}, u32[]{:S(2)}) copy-start(bf16[4,32,128,128]{3,2,1,0:T(8,128)(2,1)} %refs_20_.3) | copy-start | bytes 12582916
  37.8 1.3 %collective-permute-start.15 = (bf16[272,128]{1,0:T(8,128)(2,1)S(1)}, bf16[272,128]{1,0:T(8,128)(2,1)S(1)}, u32[]{:S(2)}, u32[]{:S(2)}) collective-permute-start(bf16[272,128]{1,0:T(8,128)(2,1)S(1)} %get-tuple-element.28), channel_id=1, source_target_pairs={{0,1},{1,0},{2,3},{3,2},{4,5},{5,4},{6,7},{7,6},{8,9},{9,8},{10,11... | collective-permute-start | bytes 208904 | tf_op jit(solution)/shard_map/ppermute | solution.py:30
  39.2 13.3 %collective-permute-start.21 = (bf16[544,128]{1,0:T(8,128)(2,1)S(1)}, bf16[544,128]{1,0:T(8,128)(2,1)S(1)}, u32[]{:S(2)}, u32[]{:S(2)}) collective-permute-start(bf16[544,128]{1,0:T(8,128)(2,1)S(1)} %constant_dynamic-update-slice_fusion.refs_0_), channel_id=1, source_target_pairs={{0,10},{1,13},{2,8},{3,15},{4,14},{5,9},{6,12},{7,11},{8,2},{9,5},... | collective-permute-start | bytes 417800 | tf_op jit(solution)/shard_map/ppermute | solution.py:30
  42.8 9.7 %collective-permute-start.19 = (bf16[544,128]{1,0:T(8,128)(2,1)S(1)}, bf16[544,128]{1,0:T(8,128)(2,1)S(1)}, u32[]{:S(2)}, u32[]{:S(2)}) collective-permute-start(bf16[544,128]{1,0:T(8,128)(2,1)S(1)} %constant_dynamic-update-slice_fusion.refs_0_), channel_id=1, source_target_pairs={{0,6},{1,9},{2,4},{3,11},{4,2},{5,13},{6,0},{7,15},{8,14},{9,1},{1... | collective-permute-start | bytes 417800 | tf_op jit(solution)/shard_map/ppermute | solution.py:30
  43.2 12.0 %collective-permute-start.17 = (bf16[544,128]{1,0:T(8,128)(2,1)S(1)}, bf16[544,128]{1,0:T(8,128)(2,1)S(1)}, u32[]{:S(2)}, u32[]{:S(2)}) collective-permute-start(bf16[544,128]{1,0:T(8,128)(2,1)S(1)} %constant_dynamic-update-slice_fusion.refs_0_), channel_id=1, source_target_pairs={{0,2},{1,5},{2,0},{3,7},{4,6},{5,1},{6,4},{7,3},{8,10},{9,13},{10,... | collective-permute-start | bytes 417800 | tf_op jit(solution)/shard_map/ppermute | solution.py:30
  44.7 11.1 %collective-permute-start.16 = (bf16[544,128]{1,0:T(8,128)(2,1)S(1)}, bf16[544,128]{1,0:T(8,128)(2,1)S(1)}, u32[]{:S(2)}, u32[]{:S(2)}) collective-permute-start(bf16[544,128]{1,0:T(8,128)(2,1)S(1)} %constant_dynamic-update-slice_fusion.refs_0_), channel_id=1, source_target_pairs={{0,14},{1,15},{2,12},{3,13},{4,10},{5,11},{6,8},{7,9},{8,6},{9,7},... | collective-permute-start | bytes 417800 | tf_op jit(solution)/shard_map/ppermute | solution.py:30
  52.5 3.3 %collective-permute-start.22 = (bf16[544,128]{1,0:T(8,128)(2,1)S(1)}, bf16[544,128]{1,0:T(8,128)(2,1)S(1)}, u32[]{:S(2)}, u32[]{:S(2)}) collective-permute-start(bf16[544,128]{1,0:T(8,128)(2,1)S(1)} %collective-permute-done.21.refs_6_), channel_id=1, source_target_pairs={{0,1},{1,0},{2,3},{3,2},{4,5},{5,4},{6,7},{7,6},{8,9},{9,8},{10,11... | collective-permute-start | bytes 417800 | tf_op jit(solution)/shard_map/ppermute | solution.py:30
  52.5 3.7 %collective-permute-start.20 = (bf16[544,128]{1,0:T(8,128)(2,1)S(1)}, bf16[544,128]{1,0:T(8,128)(2,1)S(1)}, u32[]{:S(2)}, u32[]{:S(2)}) collective-permute-start(bf16[544,128]{1,0:T(8,128)(2,1)S(1)} %collective-permute-done.19.refs_4_), channel_id=1, source_target_pairs={{0,1},{1,0},{2,3},{3,2},{4,5},{5,4},{6,7},{7,6},{8,9},{9,8},{10,11... | collective-permute-start | bytes 417800 | tf_op jit(solution)/shard_map/ppermute | solution.py:30
  55.2 1.4 %collective-permute-start.18 = (bf16[544,128]{1,0:T(8,128)(2,1)S(1)}, bf16[544,128]{1,0:T(8,128)(2,1)S(1)}, u32[]{:S(2)}, u32[]{:S(2)}) collective-permute-start(bf16[544,128]{1,0:T(8,128)(2,1)S(1)} %collective-permute-done.17.refs_2_), channel_id=1, source_target_pairs={{0,1},{1,0},{2,3},{3,2},{4,5},{5,4},{6,7},{7,6},{8,9},{9,8},{10,11... | collective-permute-start | bytes 417800 | tf_op jit(solution)/shard_map/ppermute | solution.py:30
  59.9 1.3 %collective-permute-start.23 = (bf16[144,128]{1,0:T(8,128)(2,1)S(1)}, bf16[144,128]{1,0:T(8,128)(2,1)S(1)}, u32[]{:S(2)}, u32[]{:S(2)}) collective-permute-start(bf16[144,128]{1,0:T(8,128)(2,1)S(1)} %get-tuple-element.31), channel_id=1, source_target_pairs={{0,1},{1,0},{2,3},{3,2},{4,5},{5,4},{6,7},{7,6},{8,9},{9,8},{10,11... | collective-permute-start | bytes 110600 | tf_op jit(solution)/shard_map/ppermute | solution.py:30
  61.2 8.7 %collective-permute-start.29 = (bf16[288,128]{1,0:T(8,128)(2,1)S(1)}, bf16[288,128]{1,0:T(8,128)(2,1)S(1)}, u32[]{:S(2)}, u32[]{:S(2)}) collective-permute-start(bf16[288,128]{1,0:T(8,128)(2,1)S(1)} %constant_dynamic-update-slice_fusion.2.refs_0_.refs_8_), channel_id=1, source_target_pairs={{0,10},{1,13},{2,8},{3,15},{4,14},{5,9},{6,12},{7,11},{8,2},{9,5},... | collective-permute-start | bytes 221192 | tf_op jit(solution)/shard_map/ppermute | solution.py:30
  64.7 5.4 %collective-permute-start.27 = (bf16[288,128]{1,0:T(8,128)(2,1)S(1)}, bf16[288,128]{1,0:T(8,128)(2,1)S(1)}, u32[]{:S(2)}, u32[]{:S(2)}) collective-permute-start(bf16[288,128]{1,0:T(8,128)(2,1)S(1)} %constant_dynamic-update-slice_fusion.2.refs_0_.refs_8_), channel_id=1, source_target_pairs={{0,6},{1,9},{2,4},{3,11},{4,2},{5,13},{6,0},{7,15},{8,14},{9,1},{1... | collective-permute-start | bytes 221192 | tf_op jit(solution)/shard_map/ppermute | solution.py:30
  65.5 5.2 %collective-permute-start.25 = (bf16[288,128]{1,0:T(8,128)(2,1)S(1)}, bf16[288,128]{1,0:T(8,128)(2,1)S(1)}, u32[]{:S(2)}, u32[]{:S(2)}) collective-permute-start(bf16[288,128]{1,0:T(8,128)(2,1)S(1)} %constant_dynamic-update-slice_fusion.2.refs_0_.refs_8_), channel_id=1, source_target_pairs={{0,2},{1,5},{2,0},{3,7},{4,6},{5,1},{6,4},{7,3},{8,10},{9,13},{10,... | collective-permute-start | bytes 221192 | tf_op jit(solution)/shard_map/ppermute | solution.py:30
  67.2 7.0 %collective-permute-start.24 = (bf16[288,128]{1,0:T(8,128)(2,1)S(1)}, bf16[288,128]{1,0:T(8,128)(2,1)S(1)}, u32[]{:S(2)}, u32[]{:S(2)}) collective-permute-start(bf16[288,128]{1,0:T(8,128)(2,1)S(1)} %constant_dynamic-update-slice_fusion.2.refs_0_.refs_8_), channel_id=1, source_target_pairs={{0,14},{1,15},{2,12},{3,13},{4,10},{5,11},{6,8},{7,9},{8,6},{9,7},... | collective-permute-start | bytes 221192 | tf_op jit(solution)/shard_map/ppermute | solution.py:30
  69.9 4.3 %collective-permute-start.30 = (bf16[288,128]{1,0:T(8,128)(2,1)S(1)}, bf16[288,128]{1,0:T(8,128)(2,1)S(1)}, u32[]{:S(2)}, u32[]{:S(2)}) collective-permute-start(bf16[288,128]{1,0:T(8,128)(2,1)S(1)} %collective-permute-done.29.refs_6_.refs_14_), channel_id=1, source_target_pairs={{0,1},{1,0},{2,3},{3,2},{4,5},{5,4},{6,7},{7,6},{8,9},{9,8},{10,11... | collective-permute-start | bytes 221192 | tf_op jit(solution)/shard_map/ppermute | solution.py:30
  70.0 4.2 %collective-permute-start.28 = (bf16[288,128]{1,0:T(8,128)(2,1)S(1)}, bf16[288,128]{1,0:T(8,128)(2,1)S(1)}, u32[]{:S(2)}, u32[]{:S(2)}) collective-permute-start(bf16[288,128]{1,0:T(8,128)(2,1)S(1)} %collective-permute-done.27.refs_4_.refs_12_), channel_id=1, source_target_pairs={{0,1},{1,0},{2,3},{3,2},{4,5},{5,4},{6,7},{7,6},{8,9},{9,8},{10,11... | collective-permute-start | bytes 221192 | tf_op jit(solution)/shard_map/ppermute | solution.py:30
  70.7 3.6 %collective-permute-start.26 = (bf16[288,128]{1,0:T(8,128)(2,1)S(1)}, bf16[288,128]{1,0:T(8,128)(2,1)S(1)}, u32[]{:S(2)}, u32[]{:S(2)}) collective-permute-start(bf16[288,128]{1,0:T(8,128)(2,1)S(1)} %collective-permute-done.25.refs_2_.refs_10_), channel_id=1, source_target_pairs={{0,1},{1,0},{2,3},{3,2},{4,5},{5,4},{6,7},{7,6},{8,9},{9,8},{10,11... | collective-permute-start | bytes 221192 | tf_op jit(solution)/shard_map/ppermute | solution.py:30
  77.6 1.3 %collective-permute-start.31 = (bf16[144,128]{1,0:T(8,128)(2,1)S(1)}, bf16[144,128]{1,0:T(8,128)(2,1)S(1)}, u32[]{:S(2)}, u32[]{:S(2)}) collective-permute-start(bf16[144,128]{1,0:T(8,128)(2,1)S(1)} %get-tuple-element.39), channel_id=1, source_target_pairs={{0,1},{1,0},{2,3},{3,2},{4,5},{5,4},{6,7},{7,6},{8,9},{9,8},{10,11... | collective-permute-start | bytes 110600 | tf_op jit(solution)/shard_map/ppermute | solution.py:30
  78.8 8.8 %collective-permute-start.37 = (bf16[288,128]{1,0:T(8,128)(2,1)S(1)}, bf16[288,128]{1,0:T(8,128)(2,1)S(1)}, u32[]{:S(2)}, u32[]{:S(2)}) collective-permute-start(bf16[288,128]{1,0:T(8,128)(2,1)S(1)} %constant_dynamic-update-slice_fusion.4.refs_0_.refs_16_), channel_id=1, source_target_pairs={{0,10},{1,13},{2,8},{3,15},{4,14},{5,9},{6,12},{7,11},{8,2},{9,5},... | collective-permute-start | bytes 221192 | tf_op jit(solution)/shard_map/ppermute | solution.py:30
  81.1 6.7 %collective-permute-start.35 = (bf16[288,128]{1,0:T(8,128)(2,1)S(1)}, bf16[288,128]{1,0:T(8,128)(2,1)S(1)}, u32[]{:S(2)}, u32[]{:S(2)}) collective-permute-start(bf16[288,128]{1,0:T(8,128)(2,1)S(1)} %constant_dynamic-update-slice_fusion.4.refs_0_.refs_16_), channel_id=1, source_target_pairs={{0,6},{1,9},{2,4},{3,11},{4,2},{5,13},{6,0},{7,15},{8,14},{9,1},{1... | collective-permute-start | bytes 221192 | tf_op jit(solution)/shard_map/ppermute | solution.py:30
  81.6 6.6 %collective-permute-start.33 = (bf16[288,128]{1,0:T(8,128)(2,1)S(1)}, bf16[288,128]{1,0:T(8,128)(2,1)S(1)}, u32[]{:S(2)}, u32[]{:S(2)}) collective-permute-start(bf16[288,128]{1,0:T(8,128)(2,1)S(1)} %constant_dynamic-update-slice_fusion.4.refs_0_.refs_16_), channel_id=1, source_target_pairs={{0,2},{1,5},{2,0},{3,7},{4,6},{5,1},{6,4},{7,3},{8,10},{9,13},{10,... | collective-permute-start | bytes 221192 | tf_op jit(solution)/shard_map/ppermute | solution.py:30
  82.6 7.1 %collective-permute-start.32 = (bf16[288,128]{1,0:T(8,128)(2,1)S(1)}, bf16[288,128]{1,0:T(8,128)(2,1)S(1)}, u32[]{:S(2)}, u32[]{:S(2)}) collective-permute-start(bf16[288,128]{1,0:T(8,128)(2,1)S(1)} %constant_dynamic-update-slice_fusion.4.refs_0_.refs_16_), channel_id=1, source_target_pairs={{0,14},{1,15},{2,12},{3,13},{4,10},{5,11},{6,8},{7,9},{8,6},{9,7},... | collective-permute-start | bytes 221192 | tf_op jit(solution)/shard_map/ppermute | solution.py:30
  87.6 2.0 %collective-permute-start.38 = (bf16[288,128]{1,0:T(8,128)(2,1)S(1)}, bf16[288,128]{1,0:T(8,128)(2,1)S(1)}, u32[]{:S(2)}, u32[]{:S(2)}) collective-permute-start(bf16[288,128]{1,0:T(8,128)(2,1)S(1)} %collective-permute-done.37.refs_6_.refs_22_), channel_id=1, source_target_pairs={{0,1},{1,0},{2,3},{3,2},{4,5},{5,4},{6,7},{7,6},{8,9},{9,8},{10,11... | collective-permute-start | bytes 221192 | tf_op jit(solution)/shard_map/ppermute | solution.py:30
  87.8 1.8 %collective-permute-start.36 = (bf16[288,128]{1,0:T(8,128)(2,1)S(1)}, bf16[288,128]{1,0:T(8,128)(2,1)S(1)}, u32[]{:S(2)}, u32[]{:S(2)}) collective-permute-start(bf16[288,128]{1,0:T(8,128)(2,1)S(1)} %collective-permute-done.35.refs_4_.refs_20_), channel_id=1, source_target_pairs={{0,1},{1,0},{2,3},{3,2},{4,5},{5,4},{6,7},{7,6},{8,9},{9,8},{10,11... | collective-permute-start | bytes 221192 | tf_op jit(solution)/shard_map/ppermute | solution.py:30
  88.2 1.5 %collective-permute-start.34 = (bf16[288,128]{1,0:T(8,128)(2,1)S(1)}, bf16[288,128]{1,0:T(8,128)(2,1)S(1)}, u32[]{:S(2)}, u32[]{:S(2)}) collective-permute-start(bf16[288,128]{1,0:T(8,128)(2,1)S(1)} %collective-permute-done.33.refs_2_.refs_18_), channel_id=1, source_target_pairs={{0,1},{1,0},{2,3},{3,2},{4,5},{5,4},{6,7},{7,6},{8,9},{9,8},{10,11... | collective-permute-start | bytes 221192 | tf_op jit(solution)/shard_map/ppermute | solution.py:30
  93.5 1.3 %collective-permute-start.39 = (bf16[272,128]{1,0:T(8,128)(2,1)S(1)}, bf16[272,128]{1,0:T(8,128)(2,1)S(1)}, u32[]{:S(2)}, u32[]{:S(2)}) collective-permute-start(bf16[272,128]{1,0:T(8,128)(2,1)S(1)} %get-tuple-element.47), channel_id=1, source_target_pairs={{0,1},{1,0},{2,3},{3,2},{4,5},{5,4},{6,7},{7,6},{8,9},{9,8},{10,11... | collective-permute-start | bytes 208904 | tf_op jit(solution)/shard_map/ppermute | solution.py:30
  94.8 12.7 %collective-permute-start.45 = (bf16[544,128]{1,0:T(8,128)(2,1)S(1)}, bf16[544,128]{1,0:T(8,128)(2,1)S(1)}, u32[]{:S(2)}, u32[]{:S(2)}) collective-permute-start(bf16[544,128]{1,0:T(8,128)(2,1)S(1)} %constant_dynamic-update-slice_fusion.6.refs_24_), channel_id=1, source_target_pairs={{0,10},{1,13},{2,8},{3,15},{4,14},{5,9},{6,12},{7,11},{8,2},{9,5},... | collective-permute-start | bytes 417800 | tf_op jit(solution)/shard_map/ppermute | solution.py:30
  96.3 11.2 %collective-permute-start.43 = (bf16[544,128]{1,0:T(8,128)(2,1)S(1)}, bf16[544,128]{1,0:T(8,128)(2,1)S(1)}, u32[]{:S(2)}, u32[]{:S(2)}) collective-permute-start(bf16[544,128]{1,0:T(8,128)(2,1)S(1)} %constant_dynamic-update-slice_fusion.6.refs_24_), channel_id=1, source_target_pairs={{0,6},{1,9},{2,4},{3,11},{4,2},{5,13},{6,0},{7,15},{8,14},{9,1},{1... | collective-permute-start | bytes 417800 | tf_op jit(solution)/shard_map/ppermute | solution.py:30
  98.6 12.7 %collective-permute-start.41 = (bf16[544,128]{1,0:T(8,128)(2,1)S(1)}, bf16[544,128]{1,0:T(8,128)(2,1)S(1)}, u32[]{:S(2)}, u32[]{:S(2)}) collective-permute-start(bf16[544,128]{1,0:T(8,128)(2,1)S(1)} %constant_dynamic-update-slice_fusion.6.refs_24_), channel_id=1, source_target_pairs={{0,2},{1,5},{2,0},{3,7},{4,6},{5,1},{6,4},{7,3},{8,10},{9,13},{10,... | collective-permute-start | bytes 417800 | tf_op jit(solution)/shard_map/ppermute | solution.py:30
  100.0 11.2 %collective-permute-start.40 = (bf16[544,128]{1,0:T(8,128)(2,1)S(1)}, bf16[544,128]{1,0:T(8,128)(2,1)S(1)}, u32[]{:S(2)}, u32[]{:S(2)}) collective-permute-start(bf16[544,128]{1,0:T(8,128)(2,1)S(1)} %constant_dynamic-update-slice_fusion.6.refs_24_), channel_id=1, source_target_pairs={{0,14},{1,15},{2,12},{3,13},{4,10},{5,11},{6,8},{7,9},{8,6},{9,7},... | collective-permute-start | bytes 417800 | tf_op jit(solution)/shard_map/ppermute | solution.py:30
  107.5 3.7 %collective-permute-start.46 = (bf16[544,128]{1,0:T(8,128)(2,1)S(1)}, bf16[544,128]{1,0:T(8,128)(2,1)S(1)}, u32[]{:S(2)}, u32[]{:S(2)}) collective-permute-start(bf16[544,128]{1,0:T(8,128)(2,1)S(1)} %collective-permute-done.45.refs_30_), channel_id=1, source_target_pairs={{0,1},{1,0},{2,3},{3,2},{4,5},{5,4},{6,7},{7,6},{8,9},{9,8},{10,11... | collective-permute-start | bytes 417800 | tf_op jit(solution)/shard_map/ppermute | solution.py:30
  107.5 4.7 %collective-permute-start.44 = (bf16[544,128]{1,0:T(8,128)(2,1)S(1)}, bf16[544,128]{1,0:T(8,128)(2,1)S(1)}, u32[]{:S(2)}, u32[]{:S(2)}) collective-permute-start(bf16[544,128]{1,0:T(8,128)(2,1)S(1)} %collective-permute-done.43.refs_28_), channel_id=1, source_target_pairs={{0,1},{1,0},{2,3},{3,2},{4,5},{5,4},{6,7},{7,6},{8,9},{9,8},{10,11... | collective-permute-start | bytes 417800 | tf_op jit(solution)/shard_map/ppermute | solution.py:30
  111.2 1.4 %collective-permute-start.42 = (bf16[544,128]{1,0:T(8,128)(2,1)S(1)}, bf16[544,128]{1,0:T(8,128)(2,1)S(1)}, u32[]{:S(2)}, u32[]{:S(2)}) collective-permute-start(bf16[544,128]{1,0:T(8,128)(2,1)S(1)} %collective-permute-done.41.refs_26_), channel_id=1, source_target_pairs={{0,1},{1,0},{2,3},{3,2},{4,5},{5,4},{6,7},{7,6},{8,9},{9,8},{10,11... | collective-permute-start | bytes 417800 | tf_op jit(solution)/shard_map/ppermute | solution.py:30
